TPU v7x, 32 devices: a whole 2x2x4 slice. The times are simulated.
32 devices in a mesh: group: 4 (over y, core), node: 2 (over x), gpu: 4 (over z).
Axes of the slice: x: 2, y: 2, z: 4, core: 2. Of those that a mesh axis runs over, the one named last changes fastest.
Arguments:
- tokens: bfloat16 [4096, 12288], P(('group', 'node', 'gpu')), may hold values from -6 to 6
- weight: bfloat16 [12288, 256], P(('node', 'gpu')), may hold values from -0.0546875 to 0.0546875
- grad_out: bfloat16 [4096, 256], P(('group', 'node', 'gpu')), may hold values from -0.25 to 0.25
Outputs:
- output: bfloat16 [4096, 256], P(('group', 'node', 'gpu'))
- weight_grad: float32 [12288, 256], P(('node', 'gpu'))
All inputs are finite; a program needn't handle non-finite values.
Results may differ from a plain program's by a relative error of at most 0.0029.
Values may be sent and summed in bfloat16 or wider, within the bound.
A program may use at most 128 MiB of HBM per device.

v0:
```python
import jax
import jax.numpy as jnp
from jax import lax
from jax.sharding import PartitionSpec as P


def sum_middle(received):
    return jnp.sum(received, axis=1, dtype=jnp.float32)


def local(tokens, weight, grad_out):
    tok_rows, model_width = tokens.shape
    shard_rows, out_cols = weight.shape
    projected = jnp.dot(
        tokens,
        lax.all_gather(weight, ("node", "gpu"), axis=0, tiled=True),
        preferred_element_type=jnp.float32,
    )
    local_term = lax.dot_general(
        tokens, grad_out, (((0,), (0,)), ((), ())), preferred_element_type=jnp.float32
    ).astype(jnp.bfloat16)
    stacked = local_term.reshape(model_width, 1, out_cols)
    own_shard = sum_middle(
        lax.all_to_all(stacked, ("node", "gpu"), split_axis=0, concat_axis=1, tiled=True)
    )
    output = projected.astype(jnp.bfloat16)
    weight_grad = lax.psum(own_shard, "group")
    return (output, weight_grad)


def solution(mesh):
    placed = (
        P(("group", "node", "gpu"), None),
        P(("node", "gpu"), None),
        P(("group", "node", "gpu"), None),
    )
    return jax.shard_map(
        local,
        mesh=mesh,
        in_specs=placed,
        out_specs=(P(("group", "node", "gpu"), None), P(("node", "gpu"), None)),
        check_vma=False,
    )
```

profile of v0, /device:TPU:0, one launch (start us, length us, event | category | flops | bytes accessed | tf_op | source)
XLA Modules:
  0.0 334.8 jit_solution(1449120873352739496)
XLA Ops:
  8.0 0.0 copy-start
  8.0 1.9 copy-done
  9.9 5.3 %fusion = bf16[12288,1,256]{2,0,1:T(8,128)(2,1)} fusion(bf16[128,12288]{1,0:T(8,128)(2,1)S(1)} %copy-done, bf16[128,256]{1,0:T(8,128)(2,1)} %param.5), kind=kOutput, calls=%fused_computation.1 | convolution fusion | flops 808452096 | bytes 9502720 | tf_op jit(solution)/shard_map/dot_general | solution.py:19
  15.2 0.5 broadcast
  15.7 8.9 %reduce.3 = bf16[12288,256]{1,0:T(8,128)(2,1)} reduce(bf16[12288,1,256]{2,0,1:T(8,128)(2,1)} %fusion, bf16[]{:T(256)} %broadcast), dimensions={1}, to_apply=%copy.5.reduce_sub_computation | reduce | bytes 12582914 | tf_op jit(solution)/shard_map/reshape | solution.py:22
  24.6 8.4 %reshape.13 = bf16[8,2,196608]{2,1,0:T(2,128)(2,1)} reshape(bf16[12288,256]{1,0:T(8,128)(2,1)} %reduce.3) | data formatting | bytes 12582912
  33.0 7.3 %all-to-all-start = ((bf16[8,2,196608]{2,1,0:T(2,128)(2,1)}), bf16[8,2,196608]{2,1,0:T(2,128)(2,1)}, u32[]{:S(2)}, u32[]{:S(2)}) async-start(bf16[8,2,196608]{2,1,0:T(2,128)(2,1)} %reshape.13), calls=%async_computation | async-start | bytes 12582912 | tf_op jit(solution)/shard_map/all_to_all | solution.py:24
  40.3 0.0 all-gather.2.cloned.1.call-start
  40.3 0.7 all-gather.2.cloned.1.call-update
  41.0 0.0 all-reduce.2.cloned.1.call-start
  41.1 214.5 %all-to-all-done = bf16[8,2,196608]{2,1,0:T(2,128)(2,1)} async-done(((bf16[8,2,196608]{2,1,0:T(2,128)(2,1)}), bf16[8,2,196608]{2,1,0:T(2,128)(2,1)}, u32[]{:S(2)}, u32[]{:S(2)}) %all-to-all-start) | async-done | bytes 6291488 | tf_op jit(solution)/shard_map/all_to_all | solution.py:24
  255.5 11.0 %reshape.14 = bf16[12288,1,256]{2,1,0:T(2,128)(2,1)} reshape(bf16[8,2,196608]{2,1,0:T(2,128)(2,1)} %all-to-all-done) | data formatting | bytes 12582912
  266.5 11.4 %copy.6 = f32[12288,1,256]{2,0,1:T(8,128)} copy(bf16[12288,1,256]{2,1,0:T(2,128)(2,1)} %reshape.14) | data formatting | bytes 18874368
  277.9 6.7 %reduce_sum.9 = f32[1536,256]{1,0:T(8,128)} reduce(f32[8,1536,256]{2,1,0:T(8,128)} %bitcast.7, f32[]{:T(128)} %constant.0.clone.1), dimensions={0}, to_apply=%region_0.0 | reduce | flops 2752512 | bytes 14155780 | tf_op jit(solution)/shard_map/reduce_sum | solution.py:8
  284.7 0.0 all-reduce.2.cloned.1.call-update
  284.7 0.0 all-gather.2.cloned.1.call-done
  284.7 4.4 %convolution_convert_fusion.1 = bf16[128,256]{1,0:T(8,128)(2,1)} fusion(bf16[128,12288]{1,0:T(8,128)(2,1)S(1)} %copy-done, bf16[12288,256]{1,0:T(8,128)(2,1)} %all-gather.2.cloned.1.call-done), kind=kOutput, calls=%fused_computation.2 | convolution fusion | flops 805339136 | bytes 9502720 | tf_op jit(solution)/shard_map/dot_general | solution.py:14
  289.1 35.6 %all-reduce.2.cloned.1.call-done = f32[1536,256]{1,0:T(8,128)} async-done(((f32[1536,256]{1,0:T(8,128)}), f32[1536,256]{1,0:T(8,128)}) %all-reduce.2.cloned.1.call-update) | async-done | bytes 1572880 | tf_op jit(solution)/shard_map/psum | solution.py:27
  324.7 2.7 copy.9
Async XLA Ops:
  8.0 1.9 copy-start
  33.0 222.5 %all-to-all-start = ((bf16[8,2,196608]{2,1,0:T(2,128)(2,1)}), bf16[8,2,196608]{2,1,0:T(2,128)(2,1)}, u32[]{:S(2)}, u32[]{:S(2)}) async-start(bf16[8,2,196608]{2,1,0:T(2,128)(2,1)} %reshape.13), calls=%async_computation | async-start | bytes 12582912 | tf_op jit(solution)/shard_map/all_to_all | solution.py:24
  40.3 244.4 %all-gather.2.cloned.1.call-start = ((), (), s32[]{:S(2)}) async-start(), calls=%async_computation.1 | async-start | bytes 7077888 | tf_op jit(solution)/shard_map/all_gather | solution.py:16
  41.0 283.7 %all-reduce.2.cloned.1.call-start = ((), (), s32[]{:S(2)}) async-start(), calls=%async_computation.2 | async-start | bytes 3145728 | tf_op jit(solution)/shard_map/psum | solution.py:27
Sparse Core Ops, SparseCore 0:
  43.2 204.3 all-gather.1
Sparse Core Ops, SparseCore 1:
  284.8 39.9 all-reduce.1
where the time goes:
time: 336 us; the launch traced here: 335 us
  waiting for transfers between devices  251 us (75%)
  local copies, waits for them, and re-layouts  35.8 us (11%)
  other arithmetic  15.6 us (5%)
  between operations  15.5 us (5%)
  matrix products  9.76 us (3%)
  starting transfers between devices  7.33 us (2%)
    all_to_all x1, waiting for transfers between devices, local(): lax.all_to_all(stacked, ('node', 'gpu'), split_axis=0, concat_axis=1, til...  214 us
    psum x1, waiting for transfers between devices, local(): weight_grad = lax.psum(own_shard, 'group')  35.6 us
    unnamed x6, local copies, waits for them, and re-layouts  35.3 us
    reshape x1, other arithmetic, local(): stacked = local_term.reshape(model_width, 1, out_cols)  8.88 us
    all_to_all x1, starting transfers between devices, local(): lax.all_to_all(stacked, ('node', 'gpu'), split_axis=0, concat_axis=1, til...  7.25 us
    reduce_sum x1, other arithmetic, sum_middle(): return jnp.sum(received, axis=1, dtype=jnp.float32)  6.74 us
  transfers between devices with their start and end apart: 3, of which 2 were waited for; matrix products, arithmetic and copies ran while one was open for 10% of the time, Pallas kernels for 0%

commit v1 on v0

v1 whole, which is shorter than its diff:
```python
import functools

import jax
import jax.numpy as jnp
from jax import lax
from jax.experimental import pallas as pl
from jax.experimental.pallas import tpu as pltpu
from jax.sharding import PartitionSpec as P

MESH = pl.DeviceIdType.MESH
BF16, F32 = jnp.bfloat16, jnp.float32


def kernel(Y, N, Z, K, tok, wgt, gout, out, wgrad, T, G, W, SX, RX, SZ, RZ, SY, RY, F, acc, PO, OB,
           tl, ts, tr, gl, gs, gr, wl, wr, zs, xs, ys, sx, rx, sz, rz, sy, ry, fl, fs, fr, ps, pr, ol):
    g, n, z = lax.axis_index("group"), lax.axis_index("node"), lax.axis_index("gpu")
    y, c = g // 2, g % 2
    O = N * Z
    B = tok.shape[0]
    H = T.shape[2]
    C = H // K
    Q = H // Y
    mate = (y * 2 + 1 - c, n, z)

    def xdev(e):
        return (g, lax.rem(n + e, N), z)

    def zdev(d):
        return (g, n, lax.rem(z + d, Z))

    def ydev(f):
        return (lax.rem(y + f, Y) * 2 + c, n, z)

    def own(e, d):
        return lax.rem(n + e, N) * Z + lax.rem(z + d, Z)

    def back(e, d):
        return lax.rem(n + N - e, N) * Z + lax.rem(z + Z - d, Z)

    def remote(src, dst, send, recv, dev):
        return pltpu.make_async_remote_copy(src_ref=src, dst_ref=dst, send_sem=send, recv_sem=recv,
                                            device_id=dev, device_id_type=MESH)

    mine = pl.ds(pl.multiple_of(c * B, B), B)
    order = [(e, d) for e in list(range(1, N)) + [0] for d in list(range(1, Z)) + [0]]
    pending = []

    def cols(o, half):
        return pl.ds(pl.multiple_of(o * 2 * H + half * H, 128), H)

    glocal = pltpu.make_async_copy(gout, G.at[mine, :], gl)
    glocal.start()
    tlocal = {}
    for e, d in order:
        o = own(e, d)
        tlocal[e, d] = pltpu.make_async_copy(tok.at[:, cols(o, c)], T.at[o, mine, :], tl.at[o])
        tlocal[e, d].start()
    me = own(0, 0)
    wlocal = pltpu.make_async_copy(wgt.at[pl.ds(pl.multiple_of(c * H, H), H), :], W.at[me], wl)
    wlocal.start()

    peers = [mate] + [xdev(e) for e in range(1, N)] + [zdev(d) for d in range(1, Z)] + [ydev(f) for f in range(1, Y)]
    barrier = pltpu.get_barrier_semaphore()
    for p in peers:
        pl.semaphore_signal(barrier, inc=1, device_id=p, device_id_type=MESH)
    pl.semaphore_wait(barrier, len(peers))

    gsend = remote(gout, G.at[mine, :], gs, gr, mate)
    gsend.start()
    tsend = {}
    for e, d in order:
        o = own(e, d)
        tsend[e, d] = remote(tok.at[:, cols(o, 1 - c)], T.at[o, mine, :], ts.at[o], tr.at[o], mate)
        tsend[e, d].start()

    def part(o, q):
        return W.at[o, pl.ds(pl.multiple_of(q * Q, Q), Q), :]

    wown = wgt.at[pl.ds(pl.multiple_of(c * H + y * Q, Q), Q), :]
    for d in range(1, Z):
        s = remote(wown, part(me, y), zs.at[d], wr.at[me, y], zdev(d))
        s.start()
        pending.append(s)
    for e in range(1, N):
        s = remote(wown, part(me, y), xs.at[e, 0], wr.at[me, y], xdev(e))
        s.start()
        pending.append(s)

    def arrived(o, q):
        remote(part(o, q), part(o, q), zs.at[0], wr.at[o, q], mate).wait_recv()

    def spread(o, slot):
        for f in range(1, Y):
            s = remote(part(o, y), part(o, y), ys.at[f, slot], wr.at[o, y], ydev(f))
            s.start()
            pending.append(s)

    def from_z(d):
        o = back(0, d)
        arrived(o, y)
        for e in range(1, N):
            s = remote(part(o, y), part(o, y), xs.at[e, d], wr.at[o, y], xdev(e))
            s.start()
            pending.append(s)
        spread(o, d)

    def from_x(e, d):
        o = back(e, d)
        arrived(o, y)
        spread(o, e * Z + d)

    events = [functools.partial(from_z, d) for d in range(1, Z)]
    events += [functools.partial(from_x, e, d) for e in range(1, N) for d in range(Z)]

    def rows(k):
        return pl.ds(k * C, C)

    def ready(e, d):
        tlocal[e, d].wait()
        tsend[e, d].wait_recv()

    def term(o, k):
        total = None
        for b in range(2):
            t = lax.dot_general(T[o, pl.ds(b * B, B), rows(k)], G[pl.ds(b * B, B), :],
                                (((0,), (0,)), ((), ())), preferred_element_type=F32)
            t = t.astype(BF16).astype(F32)
            total = t if total is None else total + t
        return total

    glocal.wait()
    gsend.wait_recv()
    xsend = {}
    for e in range(1, N):
        for d in list(range(1, Z)) + [0]:
            ready(e, d)
            for k in range(K):
                SX[e - 1, d, rows(k), :] = term(own(e, d), k).astype(BF16)
                s = remote(SX.at[e - 1, d, rows(k), :], RX.at[e - 1, d, rows(k), :],
                           sx.at[e - 1, d, k], rx.at[e - 1, d, k], xdev(e))
                s.start()
                xsend[e, d, k] = s
    zsend = {}
    for d in list(range(1, Z)) + [0]:
        ready(0, d)
        for k in range(K):
            total = term(own(0, d), k)
            for e in range(1, N):
                xsend[e, d, k].wait_recv()
                total = total + RX[e - 1, d, rows(k), :].astype(F32)
            if d:
                SZ[d - 1, rows(k), :] = total.astype(BF16)
                s = remote(SZ.at[d - 1, rows(k), :], RZ.at[d - 1, rows(k), :],
                           sz.at[d - 1, k], rz.at[d - 1, k], zdev(d))
                s.start()
                zsend[d, k] = s
            else:
                SY[rows(k), :] = total
            if events:
                events.pop(0)()
    for event in events:
        event()

    ysend = {}
    for k in range(K):
        total = SY[rows(k), :]
        for d in range(1, Z):
            zsend[d, k].wait_recv()
            total = total + RZ[d - 1, rows(k), :].astype(F32)
        SY[rows(k), :] = total
        for f in range(1, Y):
            s = remote(SY.at[rows(k), :], RY.at[f - 1, rows(k), :], sy.at[f - 1, k], ry.at[f - 1, k], ydev(f))
            s.start()
            ysend[f, k] = s

    wlocal.wait()
    acc[...] = jnp.dot(T[me], W[me], preferred_element_type=F32)
    for e in range(N):
        for d in range(Z):
            if e or d:
                o = back(e, d)
                for f in range(1, Y):
                    arrived(o, lax.rem(y + f, Y))
                acc[...] += jnp.dot(T[o], W[o], preferred_element_type=F32)
    theirs = pl.ds(pl.multiple_of((1 - c) * B, B), B)
    psend = remote(acc.at[theirs, :], PO, ps, pr, mate)
    psend.start()

    fsend = []
    for k in range(K):
        total = SY[rows(k), :]
        if Y == 2:
            ysend[1, k].wait_recv()
            total = total + RY[0, rows(k), :]
        elif Y > 2:
            for f in range(1, Y):
                ysend[f, k].wait_recv()
            total = jnp.zeros((C, total.shape[1]), F32)
            for q in range(Y):
                at = lax.rem(y - q + Y, Y)
                part_q = SY[rows(k), :]
                for f in range(1, Y):
                    part_q = jnp.where(at == f, RY[f - 1, rows(k), :], part_q)
                total = total + part_q
        F[rows(k), :] = total
        place = pl.ds(pl.multiple_of(c * H + k * C, C), C)
        a = pltpu.make_async_copy(F.at[rows(k), :], wgrad.at[place, :], fl.at[k])
        a.start()
        s = remote(F.at[rows(k), :], wgrad.at[place, :], fs.at[k], fr.at[k], mate)
        s.start()
        fsend.append((a, s))

    psend.wait_recv()
    OB[...] = (acc[mine, :] + PO[...]).astype(BF16)
    olocal = pltpu.make_async_copy(OB, out, ol)
    olocal.start()

    for s in pending + [gsend, psend] + list(tsend.values()) + list(xsend.values()) + list(zsend.values()) + list(ysend.values()):
        s.wait_send()
    for a, s in fsend:
        a.wait()
        s.wait()
    olocal.wait()


def fused(Y, N, Z, tokens, weight, grad_out):
    B, D = tokens.shape
    S, M = weight.shape
    H = S // 2
    K = 2
    O = N * Z
    DMA = pltpu.SemaphoreType.DMA
    scratch = [
        pltpu.VMEM((O, 2 * B, H), BF16),
        pltpu.VMEM((2 * B, M), BF16),
        pltpu.VMEM((O, H, M), BF16),
        pltpu.VMEM((N - 1, Z, H, M), BF16),
        pltpu.VMEM((N - 1, Z, H, M), BF16),
        pltpu.VMEM((Z - 1, H, M), BF16),
        pltpu.VMEM((Z - 1, H, M), BF16),
        pltpu.VMEM((H, M), F32),
        pltpu.VMEM((Y - 1, H, M), F32),
        pltpu.VMEM((H, M), F32),
        pltpu.VMEM((2 * B, M), F32),
        pltpu.VMEM((B, M), F32),
        pltpu.VMEM((B, M), BF16),
        DMA((O,)), DMA((O,)), DMA((O,)),
        DMA, DMA, DMA,
        DMA, DMA((O, Y)),
        DMA((Z,)), DMA((N, Z)), DMA((Y, O)),
        DMA((N - 1, Z, K)), DMA((N - 1, Z, K)),
        DMA((Z - 1, K)), DMA((Z - 1, K)),
        DMA((Y - 1, K)), DMA((Y - 1, K)),
        DMA((K,)), DMA((K,)), DMA((K,)),
        DMA, DMA, DMA,
    ]
    return pl.pallas_call(
        functools.partial(kernel, Y, N, Z, K),
        out_shape=(jax.ShapeDtypeStruct((B, M), BF16), jax.ShapeDtypeStruct((S, M), F32)),
        in_specs=[pl.BlockSpec(memory_space=pl.ANY)] * 3,
        out_specs=(pl.BlockSpec(memory_space=pl.ANY),) * 2,
        scratch_shapes=scratch,
        compiler_params=pltpu.CompilerParams(collective_id=0, has_side_effects=True, vmem_limit_bytes=48 * 2**20),
        cost_estimate=pl.CostEstimate(flops=4 * B * D * M, bytes_accessed=2 * B * D + 6 * S * M, transcendentals=0),
    )(tokens, weight, grad_out)


def plain(tokens, weight, grad_out):
    model_width = tokens.shape[1]
    out_cols = weight.shape[1]
    projected = jnp.dot(tokens, lax.all_gather(weight, ("node", "gpu"), axis=0, tiled=True), preferred_element_type=F32)
    term = lax.dot_general(tokens, grad_out, (((0,), (0,)), ((), ())), preferred_element_type=F32).astype(BF16)
    stacked = term.reshape(model_width, 1, out_cols)
    received = lax.all_to_all(stacked, ("node", "gpu"), split_axis=0, concat_axis=1, tiled=True)
    own_shard = jnp.sum(received, axis=1, dtype=F32)
    return projected.astype(BF16), lax.psum(own_shard, "group")


def solution(mesh):
    groups, N, Z = (mesh.shape[a] for a in ("group", "node", "gpu"))

    def local(tokens, weight, grad_out):
        half = weight.shape[0] // 2
        if groups % 2 or groups < 4 or N < 2 or Z < 2 or half % 256 or tokens.shape[0] % 128:
            return plain(tokens, weight, grad_out)
        return fused(groups // 2, N, Z, tokens, weight, grad_out)

    rows = P(("group", "node", "gpu"), None)
    owners = P(("node", "gpu"), None)
    return jax.shard_map(local, mesh=mesh, in_specs=(rows, owners, rows), out_specs=(rows, owners), check_vma=False)
```

time: 336 us -> 90.3 us (0.27)
  waiting for transfers between devices: 251 us -> 0 us
  Pallas kernels: 0 us -> 83.8 us
  local copies, waits for them, and re-layouts: 35.8 us -> 5.63 us
  other arithmetic: 15.6 us -> 0 us
  between operations: 15.5 us -> 0.65 us
  matrix products: 9.76 us -> 0 us
  starting transfers between devices: 7.33 us -> 0 us
    all_to_all x1 -> x0, waiting for transfers between devices: 214 us -> none  [local(): lax.all_to_all(stacked, ('node', 'gpu'), split_axis=0, concat_axis=1, til...]
    pallas_call x0 -> x1, Pallas kernels: none -> 83.8 us  [fused(): pl.pallas_call(functools.partial(kernel, Y, N, Z, K), out_shape=(jax.Shap...]
    psum x1 -> x0, waiting for transfers between devices: 35.6 us -> none  [local(): weight_grad = lax.psum(own_shard, 'group')]
    unnamed x6 -> x8, local copies, waits for them, and re-layouts: 35.3 us -> 5.63 us
    dot_general x2 -> x0, matrix products: 9.76 us -> none  [the longest x1 5.34 us: local(): lax.dot_general(tokens, grad_out, (((0,), (0,)), ((), ())), preferred_ele...]
    reshape x1 -> x0, other arithmetic: 8.88 us -> none  [local(): stacked = local_term.reshape(model_width, 1, out_cols)]
    all_to_all x1 -> x0, starting transfers between devices: 7.25 us -> none  [local(): lax.all_to_all(stacked, ('node', 'gpu'), split_axis=0, concat_axis=1, til...]
    reduce_sum x1 -> x0, other arithmetic: 6.74 us -> none  [sum_middle(): return jnp.sum(received, axis=1, dtype=jnp.float32)]
  transfers between devices with their start and end apart: 3 -> 0, of which waited for: 2 -> 0; matrix products, arithmetic and copies ran while one was open for 10% -> 0% of each run, Pallas kernels for 0% -> 0%
where the time goes in v1:
time: 90.3 us; the launch traced here: 90.1 us
  Pallas kernels  83.8 us (93%)
  local copies, waits for them, and re-layouts  5.63 us (6%)
    pallas_call x1, Pallas kernels, fused(): pl.pallas_call(functools.partial(kernel, Y, N, Z, K), out_shape=(jax.Shap...  83.8 us
    unnamed x8, local copies, waits for them, and re-layouts  5.63 us

profile of v1, /device:TPU:0, one launch (start us, length us, event | category | flops | bytes accessed | tf_op | source)
XLA Modules:
  0.0 90.1 jit_solution(16761001732756914290)
XLA Ops:
  0.6 0.0 copy-start
  0.6 1.9 %copy-done = bf16[128,12288]{1,0:T(8,128)(2,1)S(1)} copy-done((bf16[128,12288]{1,0:T(8,128)(2,1)S(1)}, bf16[128,12288]{1,0:T(8,128)(2,1)}, u32[]{:S(2)}) %copy-start) | copy-done | bytes 3145752
  2.5 0.0 copy-start.1
  2.5 1.1 %copy-done.1 = bf16[1536,256]{1,0:T(8,128)(2,1)S(1)} copy-done((bf16[1536,256]{1,0:T(8,128)(2,1)S(1)}, bf16[1536,256]{1,0:T(8,128)(2,1)}, u32[]{:S(2)}) %copy-start.1) | copy-done | bytes 786456
  3.7 0.0 copy-start.2
  3.7 0.8 copy-done.2
  4.5 83.8 %shard_map.50 = (bf16[128,256]{1,0:T(8,128)(2,1)S(1)}, f32[1536,256]{1,0:T(8,128)S(1)}) custom-call(bf16[128,12288]{1,0:T(8,128)(2,1)S(1)} %copy-done, bf16[1536,256]{1,0:T(8,128)(2,1)S(1)} %copy-done.1, bf16[128,256]{1,0:T(8,128)(2,1)S(1)} %copy-done.2), custom_call_target="tpu_custom_call" | custom-call | flops 1610612736 | bytes 5505024 | tf_op jit(solution)/shard_map/pallas_call | solution.py:257
  88.3 0.6 copy.7
  88.9 1.1 %copy.8 = f32[1536,256]{1,0:T(8,128)} copy(f32[1536,256]{1,0:T(8,128)S(1)} %get-tuple-element.5) | data formatting | bytes 3145728
Async XLA Ops:
  0.6 1.9 %copy-start = (bf16[128,12288]{1,0:T(8,128)(2,1)S(1)}, bf16[128,12288]{1,0:T(8,128)(2,1)}, u32[]{:S(2)}) copy-start(bf16[128,12288]{1,0:T(8,128)(2,1)} %tok.1) | copy-start | bytes 9437188
  2.5 1.1 %copy-start.1 = (bf16[1536,256]{1,0:T(8,128)(2,1)S(1)}, bf16[1536,256]{1,0:T(8,128)(2,1)}, u32[]{:S(2)}) copy-start(bf16[1536,256]{1,0:T(8,128)(2,1)} %wgt.1) | copy-start | bytes 2359300
  3.7 0.8 copy-start.2

commit v2 on v0

v2 whole, which is shorter than its diff:
```python
import functools

import jax
import jax.numpy as jnp
from jax import lax
from jax.experimental import pallas as pl
from jax.experimental.pallas import tpu as pltpu
from jax.sharding import PartitionSpec as P

MESH = pl.DeviceIdType.MESH
BF16, F32 = jnp.bfloat16, jnp.float32


def kernel(Y, N, Z, R, L, tok, wgt, gout, out, wgrad, T, G, W, SY, RY, OWN, SZ, RZ, QF, FIN, acc, PO, XS, XR, OB,
           tl, ts, tr, gl, gs, gr, wl, wr, zs, ys, sy, ry, sz, rz, fl, fy, fyr, fm, fmr, ps, pr, qs, qr, ol):
    g, n, z = lax.axis_index("group"), lax.axis_index("node"), lax.axis_index("gpu")
    y, c = g // 2, g % 2
    B = tok.shape[0]
    M = gout.shape[1]
    C = Y * L
    mate = (y * 2 + 1 - c, n, z)
    dorder = list(range(1, Z)) + [0]

    def xdev(e, j):
        core = c if j == 0 else 1 - c
        return (y * 2 + core, lax.rem(n + e, N), z)

    def zdev(d):
        return (g, n, lax.rem(z + d, Z))

    def ydev(f):
        return (lax.rem(y + f, Y) * 2 + c, n, z)

    def yat(f):
        return lax.rem(y + f, Y)

    def remote(src, dst, send, recv, dev):
        return pltpu.make_async_remote_copy(src_ref=src, dst_ref=dst, send_sem=send, recv_sem=recv,
                                            device_id=dev, device_id_type=MESH)

    def block(node, core):
        return pl.ds(pl.multiple_of((node * 2 + core) * B, B), B)

    mine = block(n, c)
    pending = []
    relations = [(e, j) for e in list(range(1, N)) + [0] for j in range(2) if e or j]

    def cols(d, r, e, core):
        o = lax.rem(n + e, N) * Z + lax.rem(z + d, Z)
        return pl.ds(pl.multiple_of(o * (2 * C * R) + r * 2 * C + core * C, 128), C)

    glocal = pltpu.make_async_copy(gout, G.at[mine, :], gl)
    glocal.start()
    tlocal, tsend = {}, {}
    for r in range(R):
        for d in dorder:
            tlocal[r, d] = pltpu.make_async_copy(tok.at[:, cols(d, r, 0, c)], T.at[d, mine, pl.ds(r * C, C)], tl.at[r, d])
            tlocal[r, d].start()
    wlocal = pltpu.make_async_copy(wgt.at[:, pl.ds(c * Y, Y)], W.at[z], wl)
    wlocal.start()

    peers = [xdev(e, j) for e, j in relations] + [zdev(d) for d in range(1, Z)] + [ydev(f) for f in range(1, Y)]
    barrier = pltpu.get_barrier_semaphore()
    for p in peers:
        pl.semaphore_signal(barrier, inc=1, device_id=p, device_id_type=MESH)
    pl.semaphore_wait(barrier, len(peers))

    gsend = {}
    for e, j in relations:
        gsend[e, j] = remote(gout, G.at[mine, :], gs.at[e, j], gr.at[e, j], xdev(e, j))
        gsend[e, j].start()

    def send_tokens(r, d):
        for e, j in relations:
            core = c if j == 0 else 1 - c
            s = remote(tok.at[:, cols(d, r, e, core)], T.at[d, mine, pl.ds(r * C, C)],
                       ts.at[r, d, e, j], tr.at[r, d, e, j], xdev(e, j))
            s.start()
            tsend[r, d, e, j] = s

    for d in dorder:
        send_tokens(0, d)

    for d in range(1, Z):
        s = remote(wgt.at[:, c * Y + y], W.at[z, :, y], zs.at[d], wr.at[z, y], zdev(d))
        s.start()
        pending.append(s)

    def arrived(o, q):
        remote(W.at[o, :, q], W.at[o, :, q], zs.at[0], wr.at[o, q], mate).wait_recv()

    def from_z(d):
        o = lax.rem(z + Z - d, Z)
        arrived(o, y)
        for f in range(1, Y):
            s = remote(W.at[o, :, y], W.at[o, :, y], ys.at[f, d], wr.at[o, y], ydev(f))
            s.start()
            pending.append(s)

    def term(r, d, q):
        total = None
        for b in range(2 * N):
            t = lax.dot_general(T[d, pl.ds(b * B, B), pl.ds(pl.multiple_of(r * C + q * L, 128), L)], G[pl.ds(b * B, B), :],
                                (((0,), (0,)), ((), ())), preferred_element_type=F32)
            t = t.astype(BF16).astype(F32)
            total = t if total is None else total + t
        return total

    ysend, zsend = {}, {}

    def terms(r, d):
        tlocal[r, d].wait()
        for e, j in relations:
            tsend[r, d, e, j].wait_recv()
        if r + 1 < R:
            send_tokens(r + 1, d)
        for f in range(1, Y):
            SY[r, d, f - 1] = term(r, d, yat(f)).astype(BF16)
            s = remote(SY.at[r, d, f - 1], RY.at[r, d, f - 1], sy.at[r, d, f - 1], ry.at[r, d, f - 1], ydev(f))
            s.start()
            ysend[r, d, f] = s
        OWN[r, d] = term(r, d, y)

    def ysum(r, d):
        total = OWN[r, d]
        for f in range(1, Y):
            ysend[r, d, f].wait_recv()
            total = total + RY[r, d, f - 1].astype(F32)
        if d:
            SZ[r, d - 1] = total.astype(BF16)
            s = remote(SZ.at[r, d - 1], RZ.at[r, d - 1], sz.at[r, d - 1], rz.at[r, d - 1], zdev(d))
            s.start()
            zsend[r, d] = s
        else:
            QF[r] = total

    finals = []
    ysent = {}

    def final(r):
        total = QF[r]
        for d in range(1, Z):
            zsend[r, d].wait_recv()
            total = total + RZ[r, d - 1].astype(F32)
        FIN[r] = total
        place = wgrad.at[r, c * Y + y]
        for f in range(1, Y):
            s = remote(FIN.at[r], place, fy.at[r, f - 1], fyr.at[r, f - 1], ydev(f))
            s.start()
            ysent[r, f] = s
        s = remote(FIN.at[r], place, fm.at[r, 0], fmr.at[r, 0], mate)
        s.start()
        finals.append(s)
        a = pltpu.make_async_copy(FIN.at[r], place, fl.at[r])
        a.start()
        locals_.append(a)

    locals_ = []

    def hand_on(r):
        for f in range(1, Y):
            ysent[r, f].wait_recv()
            place = wgrad.at[r, c * Y + lax.rem(y + Y - f, Y)]
            s = remote(place, place, fm.at[r, f], fmr.at[r, f], mate)
            s.start()
            finals.append(s)

    def project(d, first):
        o = lax.rem(z + d, Z)
        if d:
            for f in range(1, Y):
                arrived(o, yat(f))
        else:
            wlocal.wait()
        w = W[o].reshape(R * C, M)
        p = jnp.dot(T[d], w, preferred_element_type=F32)
        if first:
            acc[...] = p
        else:
            acc[...] += p

    glocal.wait()
    for e, j in relations:
        gsend[e, j].wait_recv()
    steps = [(r, d) for r in range(R) for d in dorder]
    at_step = {}
    for i, d in enumerate(range(1, Z)):
        at_step.setdefault(min(Z - 1 + i, (R - 1) * Z - 1), []).append(functools.partial(from_z, d))
    for r in range(R - 1):
        at_step.setdefault((r + 1) * Z + min(2, Z - 1), []).append(functools.partial(final, r))
        if r + 2 < R:
            at_step.setdefault((r + 2) * Z, []).append(functools.partial(hand_on, r))
    for i, (r, d) in enumerate(steps):
        terms(r, d)
        if i:
            ysum(*steps[i - 1])
        for event in at_step.get(i, []):
            event()
        if r == R - 1:
            project(d, d == dorder[0])
    psend = []
    for i in range(N):
        s = remote(acc.at[block(i, 1 - c), :], PO.at[i], ps.at[i], pr.at[i], mate)
        s.start()
        psend.append(s)
    ysum(*steps[-1])
    for s in psend:
        s.wait_recv()
    qsend = []
    for e in range(1, N):
        to = lax.rem(n + e, N)
        XS[e - 1] = acc[block(to, c), :] + PO[to]
        s = remote(XS.at[e - 1], XR.at[e - 1], qs.at[e - 1], qr.at[e - 1], xdev(e, 0))
        s.start()
        qsend.append(s)
    final(R - 1)
    if R > 1:
        hand_on(R - 2)
    total = acc[mine, :] + PO[n]
    for e in range(1, N):
        qsend[e - 1].wait_recv()
        total = total + XR[e - 1]
    OB[...] = total.astype(BF16)
    olocal = pltpu.make_async_copy(OB, out, ol)
    olocal.start()
    hand_on(R - 1)

    for s in pending + psend + qsend + [s for group in (gsend, tsend, ysend, zsend, ysent) for s in group.values()]:
        s.wait_send()
    for s in finals:
        s.wait()
    for a in locals_:
        a.wait()
    olocal.wait()


def fused(Y, N, Z, tokens, weight, grad_out):
    B, D = tokens.shape
    S, M = weight.shape
    L = 128
    R = S // (2 * Y * L)
    C = Y * L
    DMA = pltpu.SemaphoreType.DMA
    scratch = [
        pltpu.VMEM((Z, 2 * N * B, R * C), BF16),
        pltpu.VMEM((2 * N * B, M), BF16),
        pltpu.VMEM((Z, R, Y, L, M), BF16),
        pltpu.VMEM((R, Z, Y - 1, L, M), BF16),
        pltpu.VMEM((R, Z, Y - 1, L, M), BF16),
        pltpu.VMEM((R, Z, L, M), F32),
        pltpu.VMEM((R, Z - 1, L, M), BF16),
        pltpu.VMEM((R, Z - 1, L, M), BF16),
        pltpu.VMEM((R, L, M), F32),
        pltpu.VMEM((R, L, M), F32),
        pltpu.VMEM((2 * N * B, M), F32),
        pltpu.VMEM((N, B, M), F32),
        pltpu.VMEM((N - 1, B, M), F32),
        pltpu.VMEM((N - 1, B, M), F32),
        pltpu.VMEM((B, M), BF16),
        DMA((R, Z)), DMA((R, Z, N, 2)), DMA((R, Z, N, 2)),
        DMA, DMA((N, 2)), DMA((N, 2)),
        DMA, DMA((Z, Y)), DMA((Z,)), DMA((Y, Z)),
        DMA((R, Z, Y - 1)), DMA((R, Z, Y - 1)),
        DMA((R, Z - 1)), DMA((R, Z - 1)),
        DMA((R,)), DMA((R, Y - 1)), DMA((R, Y - 1)), DMA((R, Y)), DMA((R, Y)),
        DMA((N,)), DMA((N,)), DMA((N - 1,)), DMA((N - 1,)), DMA,
    ]
    output, grad = pl.pallas_call(
        functools.partial(kernel, Y, N, Z, R, L),
        out_shape=(jax.ShapeDtypeStruct((B, M), BF16), jax.ShapeDtypeStruct((R, 2 * Y, L, M), F32)),
        in_specs=[pl.BlockSpec(memory_space=pl.ANY)] * 3,
        out_specs=(pl.BlockSpec(memory_space=pl.ANY),) * 2,
        scratch_shapes=scratch,
        compiler_params=pltpu.CompilerParams(collective_id=0, has_side_effects=True, vmem_limit_bytes=61 * 2**20),
        cost_estimate=pl.CostEstimate(flops=4 * B * D * M, bytes_accessed=2 * B * D + 6 * S * M, transcendentals=0),
    )(tokens, weight.reshape(R, 2 * Y, L, M), grad_out)
    return output, grad.reshape(S, M)


def plain(tokens, weight, grad_out):
    model_width = tokens.shape[1]
    out_cols = weight.shape[1]
    projected = jnp.dot(tokens, lax.all_gather(weight, ("node", "gpu"), axis=0, tiled=True), preferred_element_type=F32)
    term = lax.dot_general(tokens, grad_out, (((0,), (0,)), ((), ())), preferred_element_type=F32).astype(BF16)
    stacked = term.reshape(model_width, 1, out_cols)
    received = lax.all_to_all(stacked, ("node", "gpu"), split_axis=0, concat_axis=1, tiled=True)
    own_shard = jnp.sum(received, axis=1, dtype=F32)
    return projected.astype(BF16), lax.psum(own_shard, "group")


def solution(mesh):
    groups, N, Z = (mesh.shape[a] for a in ("group", "node", "gpu"))

    def local(tokens, weight, grad_out):
        if groups % 2 or groups < 4 or N < 2 or Z < 2 or weight.shape[0] % (groups * 128) or tokens.shape[0] % 128:
            return plain(tokens, weight, grad_out)
        return fused(groups // 2, N, Z, tokens, weight, grad_out)

    rows = P(("group", "node", "gpu"), None)
    owners = P(("node", "gpu"), None)
    return jax.shard_map(local, mesh=mesh, in_specs=(rows, owners, rows), out_specs=(rows, owners), check_vma=False)
```

time: 336 us -> 70 us (0.21)
  waiting for transfers between devices: 251 us -> 0 us
  Pallas kernels: 0 us -> 65.1 us
  local copies, waits for them, and re-layouts: 35.8 us -> 4.12 us
  other arithmetic: 15.6 us -> 0 us
  between operations: 15.5 us -> 0.64 us
  matrix products: 9.76 us -> 0 us
  starting transfers between devices: 7.33 us -> 0 us
    all_to_all x1 -> x0, waiting for transfers between devices: 214 us -> none  [local(): lax.all_to_all(stacked, ('node', 'gpu'), split_axis=0, concat_axis=1, til...]
    pallas_call x0 -> x1, Pallas kernels: none -> 65.1 us  [fused(): pl.pallas_call(functools.partial(kernel, Y, N, Z, R, L), out_shape=(jax.S...]
    psum x1 -> x0, waiting for transfers between devices: 35.6 us -> none  [local(): weight_grad = lax.psum(own_shard, 'group')]
    unnamed x6 -> x2, local copies, waits for them, and re-layouts: 35.3 us -> 4.12 us
    dot_general x2 -> x0, matrix products: 9.76 us -> none  [the longest x1 5.34 us: local(): lax.dot_general(tokens, grad_out, (((0,), (0,)), ((), ())), preferred_ele...]
    reshape x1 -> x0, other arithmetic: 8.88 us -> none  [local(): stacked = local_term.reshape(model_width, 1, out_cols)]
    all_to_all x1 -> x0, starting transfers between devices: 7.25 us -> none  [local(): lax.all_to_all(stacked, ('node', 'gpu'), split_axis=0, concat_axis=1, til...]
    reduce_sum x1 -> x0, other arithmetic: 6.74 us -> none  [sum_middle(): return jnp.sum(received, axis=1, dtype=jnp.float32)]
  transfers between devices with their start and end apart: 3 -> 0, of which waited for: 2 -> 0; matrix products, arithmetic and copies ran while one was open for 10% -> 0% of each run, Pallas kernels for 0% -> 0%
where the time goes in v2:
time: 70 us; the launch traced here: 69.9 us
  Pallas kernels  65.1 us (93%)
  local copies, waits for them, and re-layouts  4.12 us (6%)
    pallas_call x1, Pallas kernels, fused(): pl.pallas_call(functools.partial(kernel, Y, N, Z, R, L), out_shape=(jax.S...  65.1 us
    unnamed x2, local copies, waits for them, and re-layouts  4.12 us

profile of v2, /device:TPU:0, one launch (start us, length us, event | category | flops | bytes accessed | tf_op | source)
XLA Modules:
  0.0 69.9 jit_solution(14372615321602639617)
XLA Ops:
  0.6 65.1 %shard_map.50 = (bf16[128,256]{1,0:T(8,128)(2,1)}, f32[3,4,128,256]{3,2,1,0:T(8,128)}) custom-call(bf16[128,12288]{1,0:T(8,128)(2,1)} %tok.1, bf16[3,4,128,256]{3,2,1,0:T(8,128)(2,1)} %bitcast.3, bf16[128,256]{1,0:T(8,128)(2,1)} %gout.1), custom_call_target="tpu_custom_call" | custom-call | flops 1610612736 | bytes 5505024 | tf_op jit(solution)/shard_map/pallas_call | solution.py:268
  65.7 1.5 %copy.7 = bf16[128,256]{1,0:T(8,128)(2,1)} copy(bf16[128,256]{1,0:T(8,128)(2,1)} %get-tuple-element.8) | data formatting | bytes 131072
  67.2 2.7 %copy.8 = f32[1536,256]{1,0:T(8,128)} copy(f32[1536,256]{1,0:T(8,128)} %bitcast.2) | data formatting | bytes 3145728

commit v3 on v2

--- a/solution.py
+++ b/solution.py
@@ -11,7 +11,7 @@
 BF16, F32 = jnp.bfloat16, jnp.float32
 
 
-def kernel(Y, N, Z, R, L, tok, wgt, gout, out, wgrad, T, G, W, SY, RY, OWN, SZ, RZ, QF, FIN, acc, PO, XS, XR, OB,
+def kernel(Y, N, Z, R, L, AHEAD, tok, wgt, gout, out, wgrad, T, G, GT, PT, W, SY, RY, OWN, SZ, RZ, QF, FIN, acc, PO, XS, XR, OB,
            tl, ts, tr, gl, gs, gr, wl, wr, zs, ys, sy, ry, sz, rz, fl, fy, fyr, fm, fmr, ps, pr, qs, qr, ol):
     g, n, z = lax.axis_index("group"), lax.axis_index("node"), lax.axis_index("gpu")
     y, c = g // 2, g % 2
@@ -78,8 +78,9 @@
             s.start()
             tsend[r, d, e, j] = s
 
-    for d in dorder:
-        send_tokens(0, d)
+    steps = [(r, d) for r in range(R) for d in dorder]
+    for r, d in steps[:AHEAD]:
+        send_tokens(r, d)
 
     for d in range(1, Z):
         s = remote(wgt.at[:, c * Y + y], W.at[z, :, y], zs.at[d], wr.at[z, y], zdev(d))
@@ -97,29 +98,29 @@
             s.start()
             pending.append(s)
 
-    def term(r, d, q):
-        total = None
-        for b in range(2 * N):
-            t = lax.dot_general(T[d, pl.ds(b * B, B), pl.ds(pl.multiple_of(r * C + q * L, 128), L)], G[pl.ds(b * B, B), :],
-                                (((0,), (0,)), ((), ())), preferred_element_type=F32)
-            t = t.astype(BF16).astype(F32)
-            total = t if total is None else total + t
-        return total
-
     ysend, zsend = {}, {}
 
-    def terms(r, d):
+    def ypart(q):
+        return PT[:, pl.ds(pl.multiple_of(q * L, 128), L)]
+
+    def terms(i, r, d):
         tlocal[r, d].wait()
         for e, j in relations:
             tsend[r, d, e, j].wait_recv()
-        if r + 1 < R:
-            send_tokens(r + 1, d)
-        for f in range(1, Y):
-            SY[r, d, f - 1] = term(r, d, yat(f)).astype(BF16)
+        if i + AHEAD < len(steps):
+            send_tokens(*steps[i + AHEAD])
+        total = None
+        for b in range(2 * N):
+            t = jnp.dot(GT[:, pl.ds(b * B, B)], T[d, pl.ds(b * B, B), pl.ds(r * C, C)], preferred_element_type=F32)
+            t = t.astype(BF16).astype(F32)
+            total = t if total is None else total + t
+        PT[...] = total
+        for f in range(1, Y):
+            SY[r, d, f - 1] = ypart(yat(f)).astype(BF16)
             s = remote(SY.at[r, d, f - 1], RY.at[r, d, f - 1], sy.at[r, d, f - 1], ry.at[r, d, f - 1], ydev(f))
             s.start()
             ysend[r, d, f] = s
-        OWN[r, d] = term(r, d, y)
+        OWN[r, d] = ypart(y)
 
     def ysum(r, d):
         total = OWN[r, d]
@@ -142,7 +143,7 @@
         for d in range(1, Z):
             zsend[r, d].wait_recv()
             total = total + RZ[r, d - 1].astype(F32)
-        FIN[r] = total
+        FIN[r] = total.T
         place = wgrad.at[r, c * Y + y]
         for f in range(1, Y):
             s = remote(FIN.at[r], place, fy.at[r, f - 1], fyr.at[r, f - 1], ydev(f))
@@ -165,24 +166,26 @@
             s.start()
             finals.append(s)
 
-    def project(d, first):
+    def project(d, lo, hi, first):
         o = lax.rem(z + d, Z)
-        if d:
-            for f in range(1, Y):
-                arrived(o, yat(f))
-        else:
-            wlocal.wait()
-        w = W[o].reshape(R * C, M)
-        p = jnp.dot(T[d], w, preferred_element_type=F32)
+        w = W[o, lo:hi].reshape((hi - lo) * C, M)
+        p = jnp.dot(T[d, :, lo * C:hi * C], w, preferred_element_type=F32)
         if first:
             acc[...] = p
         else:
             acc[...] += p
 
+    def weights(d):
+        if d:
+            for f in range(1, Y):
+                arrived(lax.rem(z + d, Z), yat(f))
+        else:
+            wlocal.wait()
+
     glocal.wait()
     for e, j in relations:
         gsend[e, j].wait_recv()
-    steps = [(r, d) for r in range(R) for d in dorder]
+    GT[...] = G[...].astype(F32).T.astype(BF16)
     at_step = {}
     for i, d in enumerate(range(1, Z)):
         at_step.setdefault(min(Z - 1 + i, (R - 1) * Z - 1), []).append(functools.partial(from_z, d))
@@ -191,19 +194,23 @@
         if r + 2 < R:
             at_step.setdefault((r + 2) * Z, []).append(functools.partial(hand_on, r))
     for i, (r, d) in enumerate(steps):
-        terms(r, d)
+        terms(i, r, d)
         if i:
             ysum(*steps[i - 1])
         for event in at_step.get(i, []):
             event()
         if r == R - 1:
-            project(d, d == dorder[0])
+            weights(d)
+            if R > 1:
+                project(d, 0, R - 1, d == dorder[0])
+    ysum(*steps[-1])
+    for d in dorder:
+        project(d, R - 1, R, R == 1 and d == dorder[0])
     psend = []
     for i in range(N):
         s = remote(acc.at[block(i, 1 - c), :], PO.at[i], ps.at[i], pr.at[i], mate)
         s.start()
         psend.append(s)
-    ysum(*steps[-1])
     for s in psend:
         s.wait_recv()
     qsend = []
@@ -244,13 +251,15 @@
     scratch = [
         pltpu.VMEM((Z, 2 * N * B, R * C), BF16),
         pltpu.VMEM((2 * N * B, M), BF16),
+        pltpu.VMEM((M, 2 * N * B), BF16),
+        pltpu.VMEM((M, C), F32),
         pltpu.VMEM((Z, R, Y, L, M), BF16),
-        pltpu.VMEM((R, Z, Y - 1, L, M), BF16),
-        pltpu.VMEM((R, Z, Y - 1, L, M), BF16),
-        pltpu.VMEM((R, Z, L, M), F32),
-        pltpu.VMEM((R, Z - 1, L, M), BF16),
-        pltpu.VMEM((R, Z - 1, L, M), BF16),
-        pltpu.VMEM((R, L, M), F32),
+        pltpu.VMEM((R, Z, Y - 1, M, L), BF16),
+        pltpu.VMEM((R, Z, Y - 1, M, L), BF16),
+        pltpu.VMEM((R, Z, M, L), F32),
+        pltpu.VMEM((R, Z - 1, M, L), BF16),
+        pltpu.VMEM((R, Z - 1, M, L), BF16),
+        pltpu.VMEM((R, M, L), F32),
         pltpu.VMEM((R, L, M), F32),
         pltpu.VMEM((2 * N * B, M), F32),
         pltpu.VMEM((N, B, M), F32),
@@ -266,14 +275,14 @@
         DMA((N,)), DMA((N,)), DMA((N - 1,)), DMA((N - 1,)), DMA,
     ]
     output, grad = pl.pallas_call(
-        functools.partial(kernel, Y, N, Z, R, L),
+        functools.partial(kernel, Y, N, Z, R, L, 2),
         out_shape=(jax.ShapeDtypeStruct((B, M), BF16), jax.ShapeDtypeStruct((R, 2 * Y, L, M), F32)),
-        in_specs=[pl.BlockSpec(memory_space=pl.ANY)] * 3,
+        in_specs=[pl.BlockSpec(memory_space=pltpu.HBM)] * 3,
         out_specs=(pl.BlockSpec(memory_space=pl.ANY),) * 2,
         scratch_shapes=scratch,
-        compiler_params=pltpu.CompilerParams(collective_id=0, has_side_effects=True, vmem_limit_bytes=61 * 2**20),
+        compiler_params=pltpu.CompilerParams(collective_id=0, has_side_effects=True, vmem_limit_bytes=48 * 2**20),
         cost_estimate=pl.CostEstimate(flops=4 * B * D * M, bytes_accessed=2 * B * D + 6 * S * M, transcendentals=0),
-    )(tokens, weight.reshape(R, 2 * Y, L, M), grad_out)
+    )(*(pltpu.with_memory_space_constraint(a, pltpu.HBM) for a in (tokens, weight.reshape(R, 2 * Y, L, M), grad_out)))
     return output, grad.reshape(S, M)
 
 

time: 70 us -> 67.6 us (0.966)
  local copies, waits for them, and re-layouts: 4.12 us -> 1.77 us
    unnamed x2, local copies, waits for them, and re-layouts: 4.12 us -> 1.77 us
where the time goes in v3:
time: 67.6 us; the launch traced here: 67.5 us
  Pallas kernels  65.1 us (96%)
  local copies, waits for them, and re-layouts  1.77 us (3%)
    pallas_call x1, Pallas kernels, fused(): pl.pallas_call(functools.partial(kernel, Y, N, Z, R, L, 2), out_shape=(ja...  65.1 us
    unnamed x2, local copies, waits for them, and re-layouts  1.77 us

profile of v3, /device:TPU:0, one launch (start us, length us, event | category | flops | bytes accessed | tf_op | source)
XLA Modules:
  0.0 67.5 jit_solution(3652360026358713061)
XLA Ops:
  0.6 65.1 %shard_map.50 = (bf16[128,256]{1,0:T(8,128)(2,1)S(1)}, f32[3,4,128,256]{3,2,1,0:T(8,128)S(1)}) custom-call(bf16[128,12288]{1,0:T(8,128)(2,1)} %tok.1, bf16[3,4,128,256]{3,2,1,0:T(8,128)(2,1)} %bitcast.3, bf16[128,256]{1,0:T(8,128)(2,1)} %gout.1), custom_call_target="tpu_custom_call" | custom-call | flops 1610612736 | bytes 5505024 | tf_op jit(solution)/shard_map/pallas_call | solution.py:277
  65.7 0.6 copy.7
  66.3 1.1 %copy.8 = f32[1536,256]{1,0:T(8,128)} copy(f32[1536,256]{1,0:T(8,128)S(1)} %bitcast.2) | data formatting | bytes 3145728

commit v4 on v3

--- a/solution.py
+++ b/solution.py
@@ -166,10 +166,9 @@
             s.start()
             finals.append(s)
 
-    def project(d, lo, hi, first):
-        o = lax.rem(z + d, Z)
-        w = W[o, lo:hi].reshape((hi - lo) * C, M)
-        p = jnp.dot(T[d, :, lo * C:hi * C], w, preferred_element_type=F32)
+    def project(d, first):
+        w = W[lax.rem(z + d, Z)].reshape(R * C, M)
+        p = jnp.dot(T[d], w, preferred_element_type=F32)
         if first:
             acc[...] = p
         else:
@@ -188,7 +187,7 @@
     GT[...] = G[...].astype(F32).T.astype(BF16)
     at_step = {}
     for i, d in enumerate(range(1, Z)):
-        at_step.setdefault(min(Z - 1 + i, (R - 1) * Z - 1), []).append(functools.partial(from_z, d))
+        at_step.setdefault(min(Z + 1 + i, R * Z - 1), []).append(functools.partial(from_z, d))
     for r in range(R - 1):
         at_step.setdefault((r + 1) * Z + min(2, Z - 1), []).append(functools.partial(final, r))
         if r + 2 < R:
@@ -199,13 +198,10 @@
             ysum(*steps[i - 1])
         for event in at_step.get(i, []):
             event()
-        if r == R - 1:
-            weights(d)
-            if R > 1:
-                project(d, 0, R - 1, d == dorder[0])
     ysum(*steps[-1])
-    for d in dorder:
-        project(d, R - 1, R, R == 1 and d == dorder[0])
+    for d in [0] + list(range(1, Z)):
+        weights(d)
+        project(d, d == 0)
     psend = []
     for i in range(N):
         s = remote(acc.at[block(i, 1 - c), :], PO.at[i], ps.at[i], pr.at[i], mate)
@@ -275,7 +271,7 @@
         DMA((N,)), DMA((N,)), DMA((N - 1,)), DMA((N - 1,)), DMA,
     ]
     output, grad = pl.pallas_call(
-        functools.partial(kernel, Y, N, Z, R, L, 2),
+        functools.partial(kernel, Y, N, Z, R, L, 5),
         out_shape=(jax.ShapeDtypeStruct((B, M), BF16), jax.ShapeDtypeStruct((R, 2 * Y, L, M), F32)),
         in_specs=[pl.BlockSpec(memory_space=pltpu.HBM)] * 3,
         out_specs=(pl.BlockSpec(memory_space=pl.ANY),) * 2,

time: 67.6 us -> 72.3 us (1.070)
  Pallas kernels: 65.1 us -> 69.8 us
    pallas_call x1, Pallas kernels: 65.1 us -> 69.8 us  [fused(): pl.pallas_call(functools.partial(kernel, Y, N, Z, R, L, 5), out_shape=(ja...]
where the time goes in v4:
time: 72.3 us; the launch traced here: 72.2 us
  Pallas kernels  69.8 us (97%)
  local copies, waits for them, and re-layouts  1.77 us (2%)
    pallas_call x1, Pallas kernels, fused(): pl.pallas_call(functools.partial(kernel, Y, N, Z, R, L, 5), out_shape=(ja...  69.8 us
    unnamed x2, local copies, waits for them, and re-layouts  1.77 us

profile of v4, /device:TPU:0, one launch (start us, length us, event | category | flops | bytes accessed | tf_op | source)
XLA Modules:
  0.0 72.2 jit_solution(49230858582801548)
XLA Ops:
  0.6 69.8 %shard_map.50 = (bf16[128,256]{1,0:T(8,128)(2,1)S(1)}, f32[3,4,128,256]{3,2,1,0:T(8,128)S(1)}) custom-call(bf16[128,12288]{1,0:T(8,128)(2,1)} %tok.1, bf16[3,4,128,256]{3,2,1,0:T(8,128)(2,1)} %bitcast.3, bf16[128,256]{1,0:T(8,128)(2,1)} %gout.1), custom_call_target="tpu_custom_call" | custom-call | flops 1610612736 | bytes 5505024 | tf_op jit(solution)/shard_map/pallas_call | solution.py:273
  70.4 0.6 copy.7
  71.0 1.1 %copy.8 = f32[1536,256]{1,0:T(8,128)} copy(f32[1536,256]{1,0:T(8,128)S(1)} %bitcast.2) | data formatting | bytes 3145728

commit v5 on v3

--- a/solution.py
+++ b/solution.py
@@ -11,8 +11,8 @@
 BF16, F32 = jnp.bfloat16, jnp.float32
 
 
-def kernel(Y, N, Z, R, L, AHEAD, tok, wgt, gout, out, wgrad, T, G, GT, PT, W, SY, RY, OWN, SZ, RZ, QF, FIN, acc, PO, XS, XR, OB,
-           tl, ts, tr, gl, gs, gr, wl, wr, zs, ys, sy, ry, sz, rz, fl, fy, fyr, fm, fmr, ps, pr, qs, qr, ol):
+def kernel(Y, N, Z, R, L, AHEAD, tok, wgt, gout, out, wgrad, T, XT, G, GT, PT, W, SY, RY, OWN, SZ, RZ, QF, FIN, acc, PO, XS, XR, OB,
+           tl, xl, ts, tr, gl, gs, gr, wl, wr, zs, ys, sy, ry, sz, rz, fl, fy, fyr, fm, fmr, ps, pr, qs, qr, ol):
     g, n, z = lax.axis_index("group"), lax.axis_index("node"), lax.axis_index("gpu")
     y, c = g // 2, g % 2
     B = tok.shape[0]
@@ -21,9 +21,8 @@
     mate = (y * 2 + 1 - c, n, z)
     dorder = list(range(1, Z)) + [0]
 
-    def xdev(e, j):
-        core = c if j == 0 else 1 - c
-        return (y * 2 + core, lax.rem(n + e, N), z)
+    def xdev(e):
+        return (g, lax.rem(n + e, N), z)
 
     def zdev(d):
         return (g, n, lax.rem(z + d, Z))
@@ -43,40 +42,64 @@
 
     mine = block(n, c)
     pending = []
-    relations = [(e, j) for e in list(range(1, N)) + [0] for j in range(2) if e or j]
-
-    def cols(d, r, e, core):
+
+    def cols(d, r, e, core, width):
         o = lax.rem(n + e, N) * Z + lax.rem(z + d, Z)
-        return pl.ds(pl.multiple_of(o * (2 * C * R) + r * 2 * C + core * C, 128), C)
+        return pl.ds(pl.multiple_of(o * (2 * C * R) + r * 2 * C + core * C, 128), width)
+
+    def source(e):
+        return block(lax.rem(n + N - e, N), c)
 
     glocal = pltpu.make_async_copy(gout, G.at[mine, :], gl)
     glocal.start()
     tlocal, tsend = {}, {}
     for r in range(R):
         for d in dorder:
-            tlocal[r, d] = pltpu.make_async_copy(tok.at[:, cols(d, r, 0, c)], T.at[d, mine, pl.ds(r * C, C)], tl.at[r, d])
+            tlocal[r, d] = pltpu.make_async_copy(tok.at[:, cols(d, r, 0, c, C)], T.at[d, mine, pl.ds(r * C, C)], tl.at[r, d])
             tlocal[r, d].start()
     wlocal = pltpu.make_async_copy(wgt.at[:, pl.ds(c * Y, Y)], W.at[z], wl)
     wlocal.start()
 
-    peers = [xdev(e, j) for e, j in relations] + [zdev(d) for d in range(1, Z)] + [ydev(f) for f in range(1, Y)]
+    peers = [mate] + [xdev(e) for e in range(1, N)] + [zdev(d) for d in range(1, Z)] + [ydev(f) for f in range(1, Y)]
     barrier = pltpu.get_barrier_semaphore()
     for p in peers:
         pl.semaphore_signal(barrier, inc=1, device_id=p, device_id_type=MESH)
     pl.semaphore_wait(barrier, len(peers))
 
-    gsend = {}
-    for e, j in relations:
-        gsend[e, j] = remote(gout, G.at[mine, :], gs.at[e, j], gr.at[e, j], xdev(e, j))
-        gsend[e, j].start()
+    gsend = {(0, 1): remote(gout, G.at[mine, :], gs.at[0, 1], gr.at[0, 1], mate)}
+    for e in range(1, N):
+        gsend[e, 0] = remote(gout, G.at[mine, :], gs.at[e, 0], gr.at[e, 0], xdev(e))
+    for s in gsend.values():
+        s.start()
 
     def send_tokens(r, d):
-        for e, j in relations:
-            core = c if j == 0 else 1 - c
-            s = remote(tok.at[:, cols(d, r, e, core)], T.at[d, mine, pl.ds(r * C, C)],
-                       ts.at[r, d, e, j], tr.at[r, d, e, j], xdev(e, j))
-            s.start()
-            tsend[r, d, e, j] = s
+        for e in range(1, N):
+            s = remote(tok.at[:, cols(d, r, e, 0, 2 * C)], XT.at[r, d, e - 1],
+                       ts.at[r, d, e, 0], tr.at[r, d, e, 0], xdev(e))
+            s.start()
+            tsend[r, d, e, 0] = s
+        s = remote(tok.at[:, cols(d, r, 0, 1 - c, C)], T.at[d, mine, pl.ds(r * C, C)],
+                   ts.at[r, d, 0, 1], tr.at[r, d, 0, 1], mate)
+        s.start()
+        tsend[r, d, 0, 1] = s
+
+    xlocal = {}
+
+    def take(i, r, d):
+        def half(e, core):
+            return XT.at[r, d, e - 1, :, pl.ds(pl.multiple_of(core * C, 128), C)]
+
+        for e in range(1, N):
+            tsend[r, d, e, 0].wait_recv()
+            place = T.at[d, source(e), pl.ds(r * C, C)]
+            s = remote(half(e, 1 - c), place, ts.at[r, d, e, 1], tr.at[r, d, e, 1], mate)
+            s.start()
+            tsend[r, d, e, 1] = s
+            a = pltpu.make_async_copy(half(e, c), place, xl.at[r, d, e - 1])
+            a.start()
+            xlocal[r, d, e] = a
+        if i + AHEAD < len(steps):
+            send_tokens(*steps[i + AHEAD])
 
     steps = [(r, d) for r in range(R) for d in dorder]
     for r, d in steps[:AHEAD]:
@@ -103,12 +126,12 @@
     def ypart(q):
         return PT[:, pl.ds(pl.multiple_of(q * L, 128), L)]
 
-    def terms(i, r, d):
+    def terms(r, d):
         tlocal[r, d].wait()
-        for e, j in relations:
-            tsend[r, d, e, j].wait_recv()
-        if i + AHEAD < len(steps):
-            send_tokens(*steps[i + AHEAD])
+        tsend[r, d, 0, 1].wait_recv()
+        for e in range(1, N):
+            xlocal[r, d, e].wait()
+            tsend[r, d, e, 1].wait_recv()
         total = None
         for b in range(2 * N):
             t = jnp.dot(GT[:, pl.ds(b * B, B)], T[d, pl.ds(b * B, B), pl.ds(r * C, C)], preferred_element_type=F32)
@@ -183,18 +206,27 @@
             wlocal.wait()
 
     glocal.wait()
-    for e, j in relations:
-        gsend[e, j].wait_recv()
+    for e in range(1, N):
+        gsend[e, 0].wait_recv()
+        rows = G.at[source(e), :]
+        gsend[e, 1] = remote(rows, rows, gs.at[e, 1], gr.at[e, 1], mate)
+        gsend[e, 1].start()
+    take(0, *steps[0])
+    gsend[0, 1].wait_recv()
+    for e in range(1, N):
+        gsend[e, 1].wait_recv()
     GT[...] = G[...].astype(F32).T.astype(BF16)
     at_step = {}
     for i, d in enumerate(range(1, Z)):
-        at_step.setdefault(min(Z - 1 + i, (R - 1) * Z - 1), []).append(functools.partial(from_z, d))
+        at_step.setdefault(min(1 + i, R * Z - 1), []).append(functools.partial(from_z, d))
     for r in range(R - 1):
         at_step.setdefault((r + 1) * Z + min(2, Z - 1), []).append(functools.partial(final, r))
         if r + 2 < R:
             at_step.setdefault((r + 2) * Z, []).append(functools.partial(hand_on, r))
     for i, (r, d) in enumerate(steps):
-        terms(i, r, d)
+        if i + 1 < len(steps):
+            take(i + 1, *steps[i + 1])
+        terms(r, d)
         if i:
             ysum(*steps[i - 1])
         for event in at_step.get(i, []):
@@ -217,7 +249,7 @@
     for e in range(1, N):
         to = lax.rem(n + e, N)
         XS[e - 1] = acc[block(to, c), :] + PO[to]
-        s = remote(XS.at[e - 1], XR.at[e - 1], qs.at[e - 1], qr.at[e - 1], xdev(e, 0))
+        s = remote(XS.at[e - 1], XR.at[e - 1], qs.at[e - 1], qr.at[e - 1], xdev(e))
         s.start()
         qsend.append(s)
     final(R - 1)
@@ -250,6 +282,7 @@
     DMA = pltpu.SemaphoreType.DMA
     scratch = [
         pltpu.VMEM((Z, 2 * N * B, R * C), BF16),
+        pltpu.VMEM((R, Z, N - 1, B, 2 * C), BF16),
         pltpu.VMEM((2 * N * B, M), BF16),
         pltpu.VMEM((M, 2 * N * B), BF16),
         pltpu.VMEM((M, C), F32),
@@ -266,7 +299,7 @@
         pltpu.VMEM((N - 1, B, M), F32),
         pltpu.VMEM((N - 1, B, M), F32),
         pltpu.VMEM((B, M), BF16),
-        DMA((R, Z)), DMA((R, Z, N, 2)), DMA((R, Z, N, 2)),
+        DMA((R, Z)), DMA((R, Z, N - 1)), DMA((R, Z, N, 2)), DMA((R, Z, N, 2)),
         DMA, DMA((N, 2)), DMA((N, 2)),
         DMA, DMA((Z, Y)), DMA((Z,)), DMA((Y, Z)),
         DMA((R, Z, Y - 1)), DMA((R, Z, Y - 1)),
@@ -275,7 +308,7 @@
         DMA((N,)), DMA((N,)), DMA((N - 1,)), DMA((N - 1,)), DMA,
     ]
     output, grad = pl.pallas_call(
-        functools.partial(kernel, Y, N, Z, R, L, 2),
+        functools.partial(kernel, Y, N, Z, R, L, 3),
         out_shape=(jax.ShapeDtypeStruct((B, M), BF16), jax.ShapeDtypeStruct((R, 2 * Y, L, M), F32)),
         in_specs=[pl.BlockSpec(memory_space=pltpu.HBM)] * 3,
         out_specs=(pl.BlockSpec(memory_space=pl.ANY),) * 2,

time: 67.6 us -> 68.8 us (1.018)
  Pallas kernels: 65.1 us -> 66.3 us
    pallas_call x1, Pallas kernels: 65.1 us -> 66.3 us  [fused(): pl.pallas_call(functools.partial(kernel, Y, N, Z, R, L, 3), out_shape=(ja...]
where the time goes in v5:
time: 68.8 us; the launch traced here: 68.7 us
  Pallas kernels  66.3 us (96%)
  local copies, waits for them, and re-layouts  1.77 us (3%)
    pallas_call x1, Pallas kernels, fused(): pl.pallas_call(functools.partial(kernel, Y, N, Z, R, L, 3), out_shape=(ja...  66.3 us
    unnamed x2, local copies, waits for them, and re-layouts  1.77 us

profile of v5, /device:TPU:0, one launch (start us, length us, event | category | flops | bytes accessed | tf_op | source)
XLA Modules:
  0.0 68.7 jit_solution(13574695902400069740)
XLA Ops:
  0.6 66.3 %shard_map.50 = (bf16[128,256]{1,0:T(8,128)(2,1)S(1)}, f32[3,4,128,256]{3,2,1,0:T(8,128)S(1)}) custom-call(bf16[128,12288]{1,0:T(8,128)(2,1)} %tok.1, bf16[3,4,128,256]{3,2,1,0:T(8,128)(2,1)} %bitcast.3, bf16[128,256]{1,0:T(8,128)(2,1)} %gout.1), custom_call_target="tpu_custom_call" | custom-call | flops 1610612736 | bytes 5505024 | tf_op jit(solution)/shard_map/pallas_call | solution.py:310
  66.9 0.6 copy.7
  67.5 1.1 %copy.8 = f32[1536,256]{1,0:T(8,128)} copy(f32[1536,256]{1,0:T(8,128)S(1)} %bitcast.2) | data formatting | bytes 3145728

commit v6 on v3

--- a/solution.py
+++ b/solution.py
@@ -188,7 +188,7 @@
     GT[...] = G[...].astype(F32).T.astype(BF16)
     at_step = {}
     for i, d in enumerate(range(1, Z)):
-        at_step.setdefault(min(Z - 1 + i, (R - 1) * Z - 1), []).append(functools.partial(from_z, d))
+        at_step.setdefault(min(Z - 2 + i, (R - 1) * Z - 1), []).append(functools.partial(from_z, d))
     for r in range(R - 1):
         at_step.setdefault((r + 1) * Z + min(2, Z - 1), []).append(functools.partial(final, r))
         if r + 2 < R:
@@ -204,6 +204,9 @@
             if R > 1:
                 project(d, 0, R - 1, d == dorder[0])
     ysum(*steps[-1])
+    final(R - 1)
+    if R > 1:
+        hand_on(R - 2)
     for d in dorder:
         project(d, R - 1, R, R == 1 and d == dorder[0])
     psend = []
@@ -220,9 +223,7 @@
         s = remote(XS.at[e - 1], XR.at[e - 1], qs.at[e - 1], qr.at[e - 1], xdev(e, 0))
         s.start()
         qsend.append(s)
-    final(R - 1)
-    if R > 1:
-        hand_on(R - 2)
+    hand_on(R - 1)
     total = acc[mine, :] + PO[n]
     for e in range(1, N):
         qsend[e - 1].wait_recv()
@@ -230,7 +231,6 @@
     OB[...] = total.astype(BF16)
     olocal = pltpu.make_async_copy(OB, out, ol)
     olocal.start()
-    hand_on(R - 1)
 
     for s in pending + psend + qsend + [s for group in (gsend, tsend, ysend, zsend, ysent) for s in group.values()]:
         s.wait_send()
@@ -275,7 +275,7 @@
         DMA((N,)), DMA((N,)), DMA((N - 1,)), DMA((N - 1,)), DMA,
     ]
     output, grad = pl.pallas_call(
-        functools.partial(kernel, Y, N, Z, R, L, 2),
+        functools.partial(kernel, Y, N, Z, R, L, 3),
         out_shape=(jax.ShapeDtypeStruct((B, M), BF16), jax.ShapeDtypeStruct((R, 2 * Y, L, M), F32)),
         in_specs=[pl.BlockSpec(memory_space=pltpu.HBM)] * 3,
         out_specs=(pl.BlockSpec(memory_space=pl.ANY),) * 2,

time: 67.6 us -> 67.9 us (level)
  no operation moved by 1% of the time
where the time goes in v6:
time: 67.9 us; the launch traced here: 67.7 us
  Pallas kernels  65.3 us (96%)
  local copies, waits for them, and re-layouts  1.77 us (3%)
    pallas_call x1, Pallas kernels, fused(): pl.pallas_call(functools.partial(kernel, Y, N, Z, R, L, 3), out_shape=(ja...  65.3 us
    unnamed x2, local copies, waits for them, and re-layouts  1.77 us

profile of v6, /device:TPU:0, one launch (start us, length us, event | category | flops | bytes accessed | tf_op | source)
XLA Modules:
  0.0 67.7 jit_solution(5892951576860909375)
XLA Ops:
  0.6 65.3 %shard_map.50 = (bf16[128,256]{1,0:T(8,128)(2,1)S(1)}, f32[3,4,128,256]{3,2,1,0:T(8,128)S(1)}) custom-call(bf16[128,12288]{1,0:T(8,128)(2,1)} %tok.1, bf16[3,4,128,256]{3,2,1,0:T(8,128)(2,1)} %bitcast.3, bf16[128,256]{1,0:T(8,128)(2,1)} %gout.1), custom_call_target="tpu_custom_call" | custom-call | flops 1610612736 | bytes 5505024 | tf_op jit(solution)/shard_map/pallas_call | solution.py:277
  65.9 0.6 copy.7
  66.6 1.1 %copy.8 = f32[1536,256]{1,0:T(8,128)} copy(f32[1536,256]{1,0:T(8,128)S(1)} %bitcast.2) | data formatting | bytes 3145728

commit v7 on v6

--- a/solution.py
+++ b/solution.py
@@ -82,21 +82,23 @@
     for r, d in steps[:AHEAD]:
         send_tokens(r, d)
 
-    for d in range(1, Z):
-        s = remote(wgt.at[:, c * Y + y], W.at[z, :, y], zs.at[d], wr.at[z, y], zdev(d))
-        s.start()
-        pending.append(s)
-
-    def arrived(o, q):
-        remote(W.at[o, :, q], W.at[o, :, q], zs.at[0], wr.at[o, q], mate).wait_recv()
-
-    def from_z(d):
-        o = lax.rem(z + Z - d, Z)
-        arrived(o, y)
-        for f in range(1, Y):
-            s = remote(W.at[o, :, y], W.at[o, :, y], ys.at[f, d], wr.at[o, y], ydev(f))
+    for r in range(R):
+        for d in range(1, Z):
+            s = remote(wgt.at[r, c * Y + y], W.at[z, r, y], zs.at[d, r], wr.at[z, y, r], zdev(d))
             s.start()
             pending.append(s)
+
+    def arrived(o, q, r):
+        remote(W.at[o, r, q], W.at[o, r, q], zs.at[0, r], wr.at[o, q, r], mate).wait_recv()
+
+    def from_z(r):
+        for d in range(1, Z):
+            o = lax.rem(z + Z - d, Z)
+            arrived(o, y, r)
+            for f in range(1, Y):
+                s = remote(W.at[o, r, y], W.at[o, r, y], ys.at[f, d, r], wr.at[o, y, r], ydev(f))
+                s.start()
+                pending.append(s)
 
     ysend, zsend = {}, {}
 
@@ -166,29 +168,21 @@
             s.start()
             finals.append(s)
 
-    def project(d, lo, hi, first):
-        o = lax.rem(z + d, Z)
-        w = W[o, lo:hi].reshape((hi - lo) * C, M)
-        p = jnp.dot(T[d, :, lo * C:hi * C], w, preferred_element_type=F32)
+    def project(d, first):
+        w = W[lax.rem(z + d, Z)].reshape(R * C, M)
+        p = jnp.dot(T[d], w, preferred_element_type=F32)
         if first:
             acc[...] = p
         else:
             acc[...] += p
-
-    def weights(d):
-        if d:
-            for f in range(1, Y):
-                arrived(lax.rem(z + d, Z), yat(f))
-        else:
-            wlocal.wait()
 
     glocal.wait()
     for e, j in relations:
         gsend[e, j].wait_recv()
     GT[...] = G[...].astype(F32).T.astype(BF16)
     at_step = {}
-    for i, d in enumerate(range(1, Z)):
-        at_step.setdefault(min(Z - 2 + i, (R - 1) * Z - 1), []).append(functools.partial(from_z, d))
+    for r in range(R):
+        at_step.setdefault(min(2 + r, R * Z - 1), []).append(functools.partial(from_z, r))
     for r in range(R - 1):
         at_step.setdefault((r + 1) * Z + min(2, Z - 1), []).append(functools.partial(final, r))
         if r + 2 < R:
@@ -199,16 +193,18 @@
             ysum(*steps[i - 1])
         for event in at_step.get(i, []):
             event()
-        if r == R - 1:
-            weights(d)
-            if R > 1:
-                project(d, 0, R - 1, d == dorder[0])
+        if i == len(steps) - 1:
+            wlocal.wait()
+            project(0, True)
     ysum(*steps[-1])
     final(R - 1)
     if R > 1:
         hand_on(R - 2)
-    for d in dorder:
-        project(d, R - 1, R, R == 1 and d == dorder[0])
+    for d in range(1, Z):
+        for f in range(1, Y):
+            for r in range(R):
+                arrived(lax.rem(z + d, Z), yat(f), r)
+        project(d, False)
     psend = []
     for i in range(N):
         s = remote(acc.at[block(i, 1 - c), :], PO.at[i], ps.at[i], pr.at[i], mate)
@@ -268,7 +264,7 @@
         pltpu.VMEM((B, M), BF16),
         DMA((R, Z)), DMA((R, Z, N, 2)), DMA((R, Z, N, 2)),
         DMA, DMA((N, 2)), DMA((N, 2)),
-        DMA, DMA((Z, Y)), DMA((Z,)), DMA((Y, Z)),
+        DMA, DMA((Z, Y, R)), DMA((Z, R)), DMA((Y, Z, R)),
         DMA((R, Z, Y - 1)), DMA((R, Z, Y - 1)),
         DMA((R, Z - 1)), DMA((R, Z - 1)),
         DMA((R,)), DMA((R, Y - 1)), DMA((R, Y - 1)), DMA((R, Y)), DMA((R, Y)),

time: 67.9 us -> 68 us (level)
  no operation moved by 1% of the time
where the time goes in v7:
time: 68 us; the launch traced here: 67.9 us
  Pallas kernels  65.5 us (96%)
  local copies, waits for them, and re-layouts  1.77 us (3%)
    pallas_call x1, Pallas kernels, fused(): pl.pallas_call(functools.partial(kernel, Y, N, Z, R, L, 3), out_shape=(ja...  65.5 us
    unnamed x2, local copies, waits for them, and re-layouts  1.77 us

profile of v7, /device:TPU:0, one launch (start us, length us, event | category | flops | bytes accessed | tf_op | source)
XLA Modules:
  0.0 67.9 jit_solution(18133147925410965311)
XLA Ops:
  0.6 65.5 %shard_map.50 = (bf16[128,256]{1,0:T(8,128)(2,1)S(1)}, f32[3,4,128,256]{3,2,1,0:T(8,128)S(1)}) custom-call(bf16[128,12288]{1,0:T(8,128)(2,1)} %tok.1, bf16[3,4,128,256]{3,2,1,0:T(8,128)(2,1)} %bitcast.3, bf16[128,256]{1,0:T(8,128)(2,1)} %gout.1), custom_call_target="tpu_custom_call" | custom-call | flops 1610612736 | bytes 5505024 | tf_op jit(solution)/shard_map/pallas_call | solution.py:273
  66.1 0.6 copy.7
  66.8 1.1 %copy.8 = f32[1536,256]{1,0:T(8,128)} copy(f32[1536,256]{1,0:T(8,128)S(1)} %bitcast.2) | data formatting | bytes 3145728

commit v8 on v7

--- a/solution.py
+++ b/solution.py
@@ -11,8 +11,8 @@
 BF16, F32 = jnp.bfloat16, jnp.float32
 
 
-def kernel(Y, N, Z, R, L, AHEAD, tok, wgt, gout, out, wgrad, T, G, GT, PT, W, SY, RY, OWN, SZ, RZ, QF, FIN, acc, PO, XS, XR, OB,
-           tl, ts, tr, gl, gs, gr, wl, wr, zs, ys, sy, ry, sz, rz, fl, fy, fyr, fm, fmr, ps, pr, qs, qr, ol):
+def kernel(Y, N, Z, R, L, AHEAD, tok, wgt, gout, out, wgrad, TV, T, G, GT, PT, W, SY, RY, OWN, SZ, RZ, QF, FIN, acc, PO, XS, XR, OB,
+           tv, tl, ts, tr, gl, gs, gr, wl, wr, zs, ys, sy, ry, sz, rz, fl, fy, fyr, fm, fmr, ps, pr, qs, qr, ol):
     g, n, z = lax.axis_index("group"), lax.axis_index("node"), lax.axis_index("gpu")
     y, c = g // 2, g % 2
     B = tok.shape[0]
@@ -49,6 +49,8 @@
         o = lax.rem(n + e, N) * Z + lax.rem(z + d, Z)
         return pl.ds(pl.multiple_of(o * (2 * C * R) + r * 2 * C + core * C, 128), C)
 
+    staged = pltpu.make_async_copy(tok, TV, tv)
+    staged.start()
     glocal = pltpu.make_async_copy(gout, G.at[mine, :], gl)
     glocal.start()
     tlocal, tsend = {}, {}
@@ -73,12 +75,13 @@
     def send_tokens(r, d):
         for e, j in relations:
             core = c if j == 0 else 1 - c
-            s = remote(tok.at[:, cols(d, r, e, core)], T.at[d, mine, pl.ds(r * C, C)],
+            s = remote(TV.at[:, cols(d, r, e, core)], T.at[d, mine, pl.ds(r * C, C)],
                        ts.at[r, d, e, j], tr.at[r, d, e, j], xdev(e, j))
             s.start()
             tsend[r, d, e, j] = s
 
     steps = [(r, d) for r in range(R) for d in dorder]
+    staged.wait()
     for r, d in steps[:AHEAD]:
         send_tokens(r, d)
 
@@ -245,6 +248,7 @@
     C = Y * L
     DMA = pltpu.SemaphoreType.DMA
     scratch = [
+        pltpu.VMEM((B, D), BF16),
         pltpu.VMEM((Z, 2 * N * B, R * C), BF16),
         pltpu.VMEM((2 * N * B, M), BF16),
         pltpu.VMEM((M, 2 * N * B), BF16),
@@ -262,7 +266,7 @@
         pltpu.VMEM((N - 1, B, M), F32),
         pltpu.VMEM((N - 1, B, M), F32),
         pltpu.VMEM((B, M), BF16),
-        DMA((R, Z)), DMA((R, Z, N, 2)), DMA((R, Z, N, 2)),
+        DMA, DMA((R, Z)), DMA((R, Z, N, 2)), DMA((R, Z, N, 2)),
         DMA, DMA((N, 2)), DMA((N, 2)),
         DMA, DMA((Z, Y, R)), DMA((Z, R)), DMA((Y, Z, R)),
         DMA((R, Z, Y - 1)), DMA((R, Z, Y - 1)),
@@ -271,7 +275,7 @@
         DMA((N,)), DMA((N,)), DMA((N - 1,)), DMA((N - 1,)), DMA,
     ]
     output, grad = pl.pallas_call(
-        functools.partial(kernel, Y, N, Z, R, L, 3),
+        functools.partial(kernel, Y, N, Z, R, L, 2),
         out_shape=(jax.ShapeDtypeStruct((B, M), BF16), jax.ShapeDtypeStruct((R, 2 * Y, L, M), F32)),
         in_specs=[pl.BlockSpec(memory_space=pltpu.HBM)] * 3,
         out_specs=(pl.BlockSpec(memory_space=pl.ANY),) * 2,

time: 68 us -> 68.1 us (level)
  no operation moved by 1% of the time
where the time goes in v8:
time: 68.1 us; the launch traced here: 68 us
  Pallas kernels  65.6 us (96%)
  local copies, waits for them, and re-layouts  1.77 us (3%)
    pallas_call x1, Pallas kernels, fused(): pl.pallas_call(functools.partial(kernel, Y, N, Z, R, L, 2), out_shape=(ja...  65.6 us
    unnamed x2, local copies, waits for them, and re-layouts  1.77 us

profile of v8, /device:TPU:0, one launch (start us, length us, event | category | flops | bytes accessed | tf_op | source)
XLA Modules:
  0.0 68.0 jit_solution(16658548477707784570)
XLA Ops:
  0.6 65.6 %shard_map.50 = (bf16[128,256]{1,0:T(8,128)(2,1)S(1)}, f32[3,4,128,256]{3,2,1,0:T(8,128)S(1)}) custom-call(bf16[128,12288]{1,0:T(8,128)(2,1)} %tok.1, bf16[3,4,128,256]{3,2,1,0:T(8,128)(2,1)} %bitcast.3, bf16[128,256]{1,0:T(8,128)(2,1)} %gout.1), custom_call_target="tpu_custom_call" | custom-call | flops 1610612736 | bytes 5505024 | tf_op jit(solution)/shard_map/pallas_call | solution.py:277
  66.2 0.6 copy.7
  66.9 1.1 %copy.8 = f32[1536,256]{1,0:T(8,128)} copy(f32[1536,256]{1,0:T(8,128)S(1)} %bitcast.2) | data formatting | bytes 3145728

commit v9 on v3

--- a/solution.py
+++ b/solution.py
@@ -67,8 +67,9 @@
 
     gsend = {}
     for e, j in relations:
-        gsend[e, j] = remote(gout, G.at[mine, :], gs.at[e, j], gr.at[e, j], xdev(e, j))
-        gsend[e, j].start()
+        if e == 0 or j == 0:
+            gsend[e, j] = remote(gout, G.at[mine, :], gs.at[e, j], gr.at[e, j], xdev(e, j))
+            gsend[e, j].start()
 
     def send_tokens(r, d):
         for e, j in relations:
@@ -183,8 +184,14 @@
             wlocal.wait()
 
     glocal.wait()
-    for e, j in relations:
-        gsend[e, j].wait_recv()
+    for e in range(1, N):
+        gsend[e, 0].wait_recv()
+        rows = G.at[block(lax.rem(n + N - e, N), c), :]
+        gsend[e, 1] = remote(rows, rows, gs.at[e, 1], gr.at[e, 1], mate)
+        gsend[e, 1].start()
+    gsend[0, 1].wait_recv()
+    for e in range(1, N):
+        gsend[e, 1].wait_recv()
     GT[...] = G[...].astype(F32).T.astype(BF16)
     at_step = {}
     for i, d in enumerate(range(1, Z)):

time: 67.6 us -> 66.2 us (0.979)
  Pallas kernels: 65.1 us -> 63.7 us
    pallas_call x1, Pallas kernels: 65.1 us -> 63.7 us  [fused(): pl.pallas_call(functools.partial(kernel, Y, N, Z, R, L, 2), out_shape=(ja...]
where the time goes in v9:
time: 66.2 us; the launch traced here: 66.1 us
  Pallas kernels  63.7 us (96%)
  local copies, waits for them, and re-layouts  1.77 us (3%)
    pallas_call x1, Pallas kernels, fused(): pl.pallas_call(functools.partial(kernel, Y, N, Z, R, L, 2), out_shape=(ja...  63.7 us
    unnamed x2, local copies, waits for them, and re-layouts  1.77 us

profile of v9, /device:TPU:0, one launch (start us, length us, event | category | flops | bytes accessed | tf_op | source)
XLA Modules:
  0.0 66.1 jit_solution(13136260802689125834)
XLA Ops:
  0.6 63.7 %shard_map.50 = (bf16[128,256]{1,0:T(8,128)(2,1)S(1)}, f32[3,4,128,256]{3,2,1,0:T(8,128)S(1)}) custom-call(bf16[128,12288]{1,0:T(8,128)(2,1)} %tok.1, bf16[3,4,128,256]{3,2,1,0:T(8,128)(2,1)} %bitcast.3, bf16[128,256]{1,0:T(8,128)(2,1)} %gout.1), custom_call_target="tpu_custom_call" | custom-call | flops 1610612736 | bytes 5505024 | tf_op jit(solution)/shard_map/pallas_call | solution.py:284
  64.3 0.6 copy.7
  64.9 1.1 %copy.8 = f32[1536,256]{1,0:T(8,128)} copy(f32[1536,256]{1,0:T(8,128)S(1)} %bitcast.2) | data formatting | bytes 3145728
